TPU v7x, 32 devices: a whole 2x2x4 slice. The times are simulated.
32 devices in a mesh: grp: 2 (over y), tm: 8 (over z, x), tile: 2 (over core).
Axes of the slice: x: 2, y: 2, z: 4, core: 2. Of those that a mesh axis runs over, the one named last changes fastest.
Arguments:
- vis_data: float32 [4, 128, 4, 256], P(('grp', 'tile'), 'tm'), parts along dimension 0, may hold values from -6 to 6
- vis_weight: float32 [4, 128, 256], P(('grp', 'tile'), 'tm'), parts along dimension 0, may hold values from 0.2 to 5
- kernel_taps: float32 [4, 128, 2, 8, 256], P(('grp', 'tile'), 'tm'), parts along dimension 0, may hold values from 0.2 to 1
- offsets: int32 [4, 128, 2, 256], P(('grp', 'tile'), 'tm'), parts along dimension 0, may hold values from 0 to 120
- block_patch: int32 [4, 128], P(('grp', 'tile'), 'tm'), parts along dimension 0, may hold values from 0 to 7
- block_count: int32 [4, 8], P(('grp', 'tile'), 'tm'), parts along dimension 0, may hold values from 1 to 16, 64 in all within a row
Outputs:
- image: float32 [2, 2, 8, 256, 256], P(None, None, ('grp', 'tile'), 'tm'), parts along dimension 2
There are 2 independent parts, one for each index of `grp`. A program takes and returns all parts, laid end to end along the dimension named above; each array names one. Nothing has to cross between parts.
Inputs may be any that keep to these rules, and one draw needn't show every extreme that they name: Each row of block_count sums to 64, and its largest entry is 16 in every draw.
All inputs are finite; a program needn't handle non-finite values.
Results may differ from a plain program's by a relative error of at most 0.0037.
Values sent between devices are 32-bit elements; how exact they have to be, the bound alone decides.
No kernel may reach another device: no remote copies, remote signals or barrier semaphores. Data moves between devices by JAX's collectives and lax.ppermute only.
A program may use at most 64 MiB of HBM per device.

v0:
```python
import math

import jax
import jax.numpy as jnp
import ml_dtypes
import numpy as np
from jax import lax
from jax.experimental import pallas as pl
from jax.experimental.pallas import tpu as pltpu
from jax.sharding import PartitionSpec as P

G = 256
P_SIZE = 128
K = 8
B = 256
POLS = 2
NT_C = 2
PATCHES = 4 * NT_C
GRIDS = 1 + 2 * POLS
X_ROW = 2 * K
OFF_ROW = X_ROW + GRIDS
ID_ROW = OFF_ROW + 2
ROWS = ID_ROW + 1
COUNT_LANE = 128
HIGH = lax.Precision.HIGHEST
VMEM = pl.BlockSpec(memory_space=pltpu.VMEM)
PARAMS = pltpu.CompilerParams(vmem_limit_bytes=20 * 1024 * 1024)


def pack_kernel(pieces, vis_hbm, weight_hbm, taps_hbm, offs_hbm, patch_hbm, count_ref, *refs):
    outs, scratch = refs[: len(pieces)], refs[len(pieces) :]
    vis_ref, weight_ref, taps_ref, offs_ref, patch_ref, sems = scratch
    pairs = (
        (offs_hbm, offs_ref),
        (taps_hbm, taps_ref),
        (weight_hbm, weight_ref),
        (vis_hbm, vis_ref),
        (patch_hbm, patch_ref),
    )
    copies = [pltpu.make_async_copy(a, b, sems.at[i]) for i, (a, b) in enumerate(pairs)]
    for copy in copies:
        copy.start()
    places = []
    base = 0
    for out_ref, size in zip(outs, pieces):
        places += [(out_ref, j, base + j) for j in range(size)]
        base += size
    copies[0].wait()
    copies[1].wait()
    for out_ref, j, at in places:
        for side in range(2):
            off = offs_ref[at, side : side + 1, :]
            taps = taps_ref[at, side]
            for bit in range(3):
                moved = pltpu.roll(taps, 1 << bit, 0)
                turn = jnp.broadcast_to((off >> bit) & 1, taps.shape) == 1
                taps = jnp.where(turn, moved, taps)
            out_ref[j, side * K : (side + 1) * K, :] = taps
        out_ref[j, OFF_ROW:ID_ROW, :] = offs_ref[at].astype(jnp.float32)
    copies[2].wait()
    copies[3].wait()
    for out_ref, j, at in places:
        weight = weight_ref[at : at + 1, :]
        out_ref[j, X_ROW : X_ROW + 1, :] = weight
        out_ref[j, X_ROW + 1 : OFF_ROW, :] = weight * vis_ref[at]
    copies[4].wait()
    lane = lax.broadcasted_iota(jnp.int32, (1, B), 1)
    for out_ref, j, at in places:
        live = jnp.clip(count_ref[0, 0] - (at - j), 0, out_ref.shape[0])
        row = jnp.where(lane < COUNT_LANE, patch_ref[0, at], live)
        out_ref[j, ID_ROW:ROWS, :] = row.astype(jnp.float32)


def pack(pieces, vis, weight, taps, offs, patches, count):
    arrays = (vis, weight, taps, offs, patches)
    spaces = [pltpu.VMEM] * 4 + [pltpu.SMEM]
    hbm, smem = pl.BlockSpec(memory_space=pltpu.HBM), pl.BlockSpec(memory_space=pltpu.SMEM)
    return pl.pallas_call(
        lambda *refs: pack_kernel(pieces, *refs),
        out_shape=[jax.ShapeDtypeStruct((size, ROWS, B), jnp.float32) for size in pieces],
        in_specs=[hbm] * 5 + [smem],
        out_specs=[VMEM] * len(pieces),
        scratch_shapes=[space(a.shape, a.dtype) for space, a in zip(spaces, arrays)] + [pltpu.SemaphoreType.DMA((5,))],
        compiler_params=PARAMS,
        name="pack",
    )(*[pltpu.with_memory_space_constraint(a, pltpu.HBM) for a in arrays], count)


def spread(off):
    row = lax.broadcasted_iota(jnp.int32, (16, B), 0)
    gap = off.astype(jnp.int32) - row
    step = (gap + 15) >> 4
    inside = (step << 4) - gap < K
    return jnp.where(inside, step, -1).astype(jnp.float32).astype(jnp.bfloat16)


def block_factors(block, live):
    rows_u = jnp.concatenate([block[0:K]] * 2, axis=0)
    rows_v = jnp.concatenate([block[K : 2 * K]] * 2, axis=0)
    step_u = spread(block[OFF_ROW : OFF_ROW + 1])
    step_v = spread(block[OFF_ROW + 1 : OFF_ROW + 2])
    if live is not None:
        rows_v = jnp.where(live, rows_v, 0.0)
    rows_v = rows_v.astype(jnp.bfloat16)
    zero = jnp.zeros((16, B), jnp.bfloat16)
    steps = P_SIZE // 16
    right = jnp.concatenate([jnp.where(step_v == s, rows_v, zero) for s in range(steps)], axis=0)
    hits = [step_u == s for s in range(steps)]
    left = []
    for e in range(GRIDS):
        product = (rows_u * block[X_ROW + e : X_ROW + e + 1]).astype(jnp.bfloat16)
        left += [jnp.where(hit, product, zero) for hit in hits]
    return jnp.concatenate(left, axis=0), right


def add_some(buf_ref, acc_ref, first, count, unroll):
    waiting = None
    for i in range(unroll):
        j = first if i == 0 else jnp.minimum(first + i, buf_ref.shape[0] - 1)
        block = buf_ref[j]
        left, right = block_factors(block, None if i == 0 else first + i < count)
        patch = lax.dot_general(
            right, left, (((1,), (1,)), ((), ())), preferred_element_type=jnp.float32
        )
        if waiting is not None:
            acc_ref[waiting[0]] += waiting[1]
        waiting = block[ID_ROW:ROWS, 0:1][0, 0].astype(jnp.int32), patch
    acc_ref[waiting[0]] += waiting[1]


def grid_kernel(n, first, last, *refs):
    bufs = refs[:n]
    acc_ref = refs[n] if first else refs[n + 1]
    if first:
        acc_ref[...] = jnp.zeros_like(acc_ref)
    for buf_ref in bufs:
        count = buf_ref[0, ID_ROW:ROWS, COUNT_LANE : COUNT_LANE + 1][0, 0].astype(jnp.int32)

        tall = (count + 3) // 8

        def eight(step, _, buf_ref=buf_ref, count=count):
            add_some(buf_ref, acc_ref, 8 * step, count, 8)
            return 0

        lax.fori_loop(0, tall, eight, 0)

        @pl.when(count > 8 * tall)
        def _(buf_ref=buf_ref, count=count, tall=tall):
            add_some(buf_ref, acc_ref, 8 * tall, count, 4)

    if last:
        sums_ref = refs[-1]
        dens = acc_ref[:, :, :P_SIZE]
        for i, value in enumerate((dens, dens * dens)):
            part = jnp.sum(value.reshape(-1, 8, P_SIZE), axis=0)
            part = jnp.sum(jnp.sum(part, axis=0, keepdims=True), axis=1, keepdims=True)
            sums_ref[8 * i : 8 * i + 8, :] = jnp.broadcast_to(part, (8, P_SIZE))


def add_blocks(acc, bufs, last=False):
    first = acc is None
    n = len(bufs)
    slots = sum(buf.shape[0] for buf in bufs)
    out_shape = [jax.ShapeDtypeStruct((PATCHES, P_SIZE, GRIDS * P_SIZE), jnp.float32)]
    if last:
        out_shape.append(jax.ShapeDtypeStruct((16, P_SIZE), jnp.float32))
    args = list(bufs) + ([] if first else [acc])
    flops = 4 * slots * GRIDS * P_SIZE * P_SIZE * B
    out = pl.pallas_call(
        lambda *refs: grid_kernel(n, first, last, *refs),
        out_shape=out_shape,
        in_specs=[VMEM] * len(args),
        out_specs=[VMEM] * len(out_shape),
        input_output_aliases={} if first else {n: 0},
        compiler_params=PARAMS,
        cost_estimate=pl.CostEstimate(flops=flops, bytes_accessed=slots * ROWS * B, transcendentals=0),
        name="grid",
    )(*args)
    return tuple(out) if last else out[0]


def two_parts(value):
    high = value.astype(jnp.bfloat16)
    return high, (value - high.astype(jnp.float32)).astype(jnp.bfloat16)


def image_kernel(acc_ref, mine_ref, other_ref, row_ref, col_ref, out_ref):
    s1 = mine_ref[0:1, :] + other_ref[0:1, :]
    s2 = mine_ref[8:9, :] + other_ref[8:9, :]
    factor = 2.5 * s1 / s2
    width = out_ref.shape[3]
    half = 2 * width
    done = []
    for t in range(NT_C):
        tiles = [[acc_ref.at[4 * t + 2 * pr + pc] for pr in range(2)] for pc in range(2)]
        weights = [[1.0 / (1.0 + factor * tile[:, :P_SIZE]) for tile in pair] for pair in tiles]
        for pol in range(POLS):
            cells = []
            for e in (1 + 2 * pol, 2 + 2 * pol):
                for pc in range(2):
                    strip = [
                        tiles[pc][pr][:, e * P_SIZE : (e + 1) * P_SIZE] * weights[pc][pr] for pr in range(2)
                    ]
                    cells.append(jnp.concatenate(strip, axis=1))
            high, low = two_parts(jnp.concatenate(cells, axis=0))
            both = jnp.dot(row_ref[...], high, preferred_element_type=jnp.float32)
            rest = jnp.dot(row_ref[:half], low, preferred_element_type=jnp.float32)
            done.append(both[:half] + both[half:] + rest)
    high, low = two_parts(jnp.concatenate(done, axis=0))
    both = jnp.dot(high, col_ref[...], preferred_element_type=jnp.float32)
    rest = jnp.dot(low, col_ref[:, : 2 * G], preferred_element_type=jnp.float32)
    done = both[:, : 2 * G] + both[:, 2 * G :] + rest
    for t in range(NT_C):
        for pol in range(POLS):
            at = (t * POLS + pol) * half
            real, imag = done[at : at + width], done[at + width : at + half]
            out_ref[pol, 0, t] = real[:, :G] + imag[:, G:]
            out_ref[pol, 1, t] = imag[:, :G] - real[:, G:]


def make_image(acc, mine, other, row_table, col_table, width):
    return pl.pallas_call(
        image_kernel,
        out_shape=jax.ShapeDtypeStruct((POLS, 2, NT_C, width, G), jnp.float32),
        in_specs=[VMEM] * 5,
        out_specs=VMEM,
        compiler_params=PARAMS,
        name="image",
    )(acc, mine, other, row_table, col_table)


def dft_tables():
    index = np.arange(G)
    phase = (index[:, None] * index[None, :] % G) * (2.0 * math.pi / G)
    return np.cos(phase).astype(np.float32), np.sin(phase).astype(np.float32)


def np_parts(table, axis):
    high = table.astype(ml_dtypes.bfloat16)
    low = (table - high.astype(np.float32)).astype(ml_dtypes.bfloat16)
    return np.concatenate([high, low], axis=axis)


def image_tables(n_tm):
    cosine, sine = dft_tables()
    rows = []
    for cos_part, sin_part in zip(np.split(cosine, n_tm, axis=1), np.split(sine, n_tm, axis=1)):
        rows.append(np_parts(np.block([[cos_part, -sin_part], [sin_part, cos_part]]).T, 0))
    return np.stack(rows), np_parts(np.concatenate([cosine, sine], axis=1) / G, 1)


def by_gather(packed, n_tm):
    order = list(range(0, n_tm, 2)) + list(range(1, n_tm, 2))[::-1]
    up = [(order[i], order[(i + 1) % n_tm]) for i in range(n_tm)]
    down = [(b, a) for a, b in up]

    def both_ways(pair):
        return [lax.ppermute(pair[0], "tm", up), lax.ppermute(pair[1], "tm", down)]

    leading = both_ways(packed)
    trailing = both_ways(packed[::-1])
    acc = add_blocks(None, packed)
    for step in range(2, n_tm // 2 + 1):
        following = both_ways(leading)
        acc = add_blocks(acc, leading)
        acc, *trailing = lax.optimization_barrier((acc, *trailing))
        leading = following
        following = both_ways(trailing) if step < n_tm // 2 else None
        acc = add_blocks(acc, trailing)
        trailing = following
    acc = add_blocks(acc, leading[:1])
    return add_blocks(acc, leading[1:], last=True)


def rest_by_rows(acc, cosine, sine):
    grid = acc.reshape(NT_C, 2, 2, P_SIZE, GRIDS, P_SIZE)
    flat = jnp.transpose(grid, (4, 0, 1, 5, 2, 3)).reshape(GRIDS, NT_C * G, G)
    owned = lax.psum_scatter(flat, "tm", scatter_dimension=1, tiled=True)
    dens = owned[0]
    totals = lax.psum((jnp.sum(dens), jnp.sum(dens * dens)), ("tm", "tile"))
    factor = 2.5 * totals[0] / totals[1]
    weighted = owned[1:] / (1.0 + factor * dens[None])
    weighted = weighted.reshape(POLS, 2, dens.shape[0], G)
    real, imag = weighted[:, 0], weighted[:, 1]

    def rows(a, b):
        return jnp.einsum("prj,jn->prn", a, b, precision=HIGH)

    done = jnp.stack([rows(real, cosine) + rows(imag, sine), rows(imag, cosine) - rows(real, sine)], axis=1)
    width = G // lax.axis_size("tm")
    every_row = lax.all_gather(done, "tm", axis=2, tiled=True)
    columns = lax.dynamic_slice_in_dim(every_row, lax.axis_index("tm") * width, width, 3)
    columns = columns.reshape(POLS, 2, NT_C, G, width)
    real, imag = columns[:, 0], columns[:, 1]

    def cols(a, b):
        return jnp.einsum("mi,ptic->ptcm", a, b, precision=HIGH)

    out = jnp.stack([cols(cosine, real) + cols(sine, imag), cols(cosine, imag) - cols(sine, real)], axis=1)
    return out / G


def body(vis_data, vis_weight, kernel_taps, offsets, block_patch, block_count):
    slots = vis_weight.shape[1]
    n_tm = lax.axis_size("tm")
    pieces = (slots // 2, slots - slots // 2)
    packed = pack(pieces, vis_data[0], vis_weight[0], kernel_taps[0], offsets[0], block_patch, block_count)
    if n_tm > 8:
        cosine, sine = dft_tables()
        return rest_by_rows(add_blocks(None, packed), jnp.asarray(cosine), jnp.asarray(sine))
    acc, mine = by_gather(packed, n_tm)
    n_tile = lax.axis_size("tile")
    other = lax.ppermute(mine, "tile", [(i, n_tile - 1 - i) for i in range(n_tile)])
    row_tables, col_table = image_tables(n_tm)
    row_table = lax.dynamic_index_in_dim(jnp.asarray(row_tables), lax.axis_index("tm"), 0, keepdims=False)
    return make_image(acc, mine, other, row_table, jnp.asarray(col_table), G // n_tm)


def solution(mesh):
    return jax.shard_map(
        body,
        mesh=mesh,
        in_specs=(
            P(("grp", "tile"), "tm", None, None),
            P(("grp", "tile"), "tm", None),
            P(("grp", "tile"), "tm", None, None, None),
            P(("grp", "tile"), "tm", None, None),
            P(("grp", "tile"), "tm"),
            P(("grp", "tile"), "tm"),
        ),
        out_specs=P(None, None, ("grp", "tile"), "tm", None),
        check_vma=False,
    )
```

profile of v0, /device:TPU:1, one launch (start us, length us, event | category | flops | bytes accessed | tf_op | source)
XLA Modules:
  0.0 41.0 jit_solution(8849158174306870238)
XLA Ops:
  0.7 1.2 %pack.1 = (f32[8,24,256]{2,1,0:T(8,128)S(1)}, f32[8,24,256]{2,1,0:T(8,128)S(1)}) custom-call(f32[16,4,256]{2,1,0:T(4,128)} %bitcast.7, f32[16,256]{1,0:T(8,128)} %bitcast.9, f32[16,2,8,256]{3,2,1,0:T(8,128)} %bitcast.6, s32[16,2,256]{2,1,0:T(2,128)} %bitcast.8, s32[1,16]{1,0:T(1,128)} %refs_4_.1, s32[1,1]{1,0:T(1,128)S(6)} %copy.25.refs_5_), custom_call_target="tpu_custom_call" | custom-call | tf_op jit(solution)/shard_map/pack/pallas_call | solution.py:78
  1.9 2.1 %collective-permute-start = (f32[8,24,256]{2,1,0:T(8,128)S(1)}, f32[8,24,256]{2,1,0:T(8,128)S(1)}, u32[]{:S(2)}, u32[]{:S(2)}) collective-permute-start(f32[8,24,256]{2,1,0:T(8,128)S(1)} %get-tuple-element.18.refs_1_), channel_id=1, source_target_pairs={{4,0},{8,4},{12,8},{14,12},{10,14},{6,10},{2,6},{0,2},{5,1},{9,5},... | collective-permute-start | bytes 589832 | tf_op jit(solution)/shard_map/ppermute | solution.py:258
  4.0 0.2 collective-permute-start.4
  4.1 1.4 %collective-permute-start.8 = (f32[8,24,256]{2,1,0:T(8,128)S(1)}, f32[8,24,256]{2,1,0:T(8,128)S(1)}, u32[]{:S(2)}, u32[]{:S(2)}) collective-permute-start(f32[8,24,256]{2,1,0:T(8,128)S(1)} %get-tuple-element.18.refs_1_), channel_id=1, source_target_pairs={{0,4},{4,8},{8,12},{12,14},{14,10},{10,6},{6,2},{2,0},{1,5},{5,9},... | collective-permute-start | bytes 589832 | tf_op jit(solution)/shard_map/ppermute | solution.py:258
  5.5 0.1 collective-permute-start.9
  5.6 1.2 %grid.9.refs_2_ = f32[8,128,640]{2,1,0:T(8,128)S(1)} custom-call(f32[8,24,256]{2,1,0:T(8,128)S(1)} %get-tuple-element.19.refs_0_, f32[8,24,256]{2,1,0:T(8,128)S(1)} %get-tuple-element.18.refs_1_), custom_call_target="tpu_custom_call" | custom-call | flops 1342177280 | bytes 98304 | tf_op jit(solution)/shard_map/grid/pallas_call | solution.py:169
  6.8 1.9 %collective-permute-done.refs_1_ = f32[8,24,256]{2,1,0:T(8,128)S(1)} collective-permute-done((f32[8,24,256]{2,1,0:T(8,128)S(1)}, f32[8,24,256]{2,1,0:T(8,128)S(1)}, u32[]{:S(2)}, u32[]{:S(2)}) %collective-permute-start) | collective-permute-done | bytes 196640 | tf_op jit(solution)/shard_map/ppermute | solution.py:258
  8.7 1.1 %collective-permute-start.1 = (f32[8,24,256]{2,1,0:T(8,128)S(1)}, f32[8,24,256]{2,1,0:T(8,128)S(1)}, u32[]{:S(2)}, u32[]{:S(2)}) collective-permute-start(f32[8,24,256]{2,1,0:T(8,128)S(1)} %collective-permute-done.refs_1_), channel_id=1, source_target_pairs={{4,0},{8,4},{12,8},{14,12},{10,14},{6,10},{2,6},{0,2},{5,1},{9,5},... | collective-permute-start | bytes 589832 | tf_op jit(solution)/shard_map/ppermute | solution.py:258
  9.7 0.0 collective-permute-done.4.refs_0_
  9.7 0.4 collective-permute-start.5
  10.1 2.0 %grid.10.refs_2_ = f32[8,128,640]{2,1,0:T(8,128)S(1)} custom-call(f32[8,24,256]{2,1,0:T(8,128)S(1)} %collective-permute-done.4.refs_0_, f32[8,24,256]{2,1,0:T(8,128)S(1)} %collective-permute-done.refs_1_, f32[8,128,640]{2,1,0:T(8,128)S(1)} %grid.9.refs_2_), custom_call_target="tpu_custom_call", output_to_operand_aliasing={{}: (2, {})} | custom-call | flops 1342177280 | bytes 98304 | tf_op jit(solution)/shard_map/grid/pallas_call | solution.py:169
  12.2 1.5 %collective-permute-done.8.refs_0_ = f32[8,24,256]{2,1,0:T(8,128)S(1)} collective-permute-done((f32[8,24,256]{2,1,0:T(8,128)S(1)}, f32[8,24,256]{2,1,0:T(8,128)S(1)}, u32[]{:S(2)}, u32[]{:S(2)}) %collective-permute-start.8) | collective-permute-done | bytes 196640 | tf_op jit(solution)/shard_map/ppermute | solution.py:258
  13.6 0.0 collective-permute-done.9.refs_1_
  13.6 0.5 %collective-permute-start.10 = (f32[8,24,256]{2,1,0:T(8,128)S(1)}, f32[8,24,256]{2,1,0:T(8,128)S(1)}, u32[]{:S(2)}, u32[]{:S(2)}) collective-permute-start(f32[8,24,256]{2,1,0:T(8,128)S(1)} %collective-permute-done.8.refs_0_), channel_id=1, source_target_pairs={{0,4},{4,8},{8,12},{12,14},{14,10},{10,6},{6,2},{2,0},{1,5},{5,9},... | collective-permute-start | bytes 589832 | tf_op jit(solution)/shard_map/ppermute | solution.py:258
  14.1 1.0 %collective-permute-start.11 = (f32[8,24,256]{2,1,0:T(8,128)S(1)}, f32[8,24,256]{2,1,0:T(8,128)S(1)}, u32[]{:S(2)}, u32[]{:S(2)}) collective-permute-start(f32[8,24,256]{2,1,0:T(8,128)S(1)} %collective-permute-done.9.refs_1_), channel_id=1, source_target_pairs={{4,0},{8,4},{12,8},{14,12},{10,14},{6,10},{2,6},{0,2},{5,1},{9,5},... | collective-permute-start | bytes 589832 | tf_op jit(solution)/shard_map/ppermute | solution.py:258
  15.1 1.6 %grid.11.refs_2_ = f32[8,128,640]{2,1,0:T(8,128)S(1)} custom-call(f32[8,24,256]{2,1,0:T(8,128)S(1)} %collective-permute-done.8.refs_0_, f32[8,24,256]{2,1,0:T(8,128)S(1)} %collective-permute-done.9.refs_1_, f32[8,128,640]{2,1,0:T(8,128)S(1)} %grid.10.refs_2_), custom_call_target="tpu_custom_call", output_to_operand_aliasing={{}: (2, {})} | custom-call | flops 1342177280 | bytes 98304 | tf_op jit(solution)/shard_map/grid/pallas_call | solution.py:169
  16.7 0.4 collective-permute-done.1.refs_1_
  17.1 1.1 %collective-permute-start.2 = (f32[8,24,256]{2,1,0:T(8,128)S(1)}, f32[8,24,256]{2,1,0:T(8,128)S(1)}, u32[]{:S(2)}, u32[]{:S(2)}) collective-permute-start(f32[8,24,256]{2,1,0:T(8,128)S(1)} %collective-permute-done.1.refs_1_), channel_id=1, source_target_pairs={{4,0},{8,4},{12,8},{14,12},{10,14},{6,10},{2,6},{0,2},{5,1},{9,5},... | collective-permute-start | bytes 589832 | tf_op jit(solution)/shard_map/ppermute | solution.py:258
  18.2 0.0 collective-permute-done.5.refs_0_
  18.2 0.4 %collective-permute-start.6 = (f32[8,24,256]{2,1,0:T(8,128)S(1)}, f32[8,24,256]{2,1,0:T(8,128)S(1)}, u32[]{:S(2)}, u32[]{:S(2)}) collective-permute-start(f32[8,24,256]{2,1,0:T(8,128)S(1)} %collective-permute-done.5.refs_0_), channel_id=1, source_target_pairs={{0,4},{4,8},{8,12},{12,14},{14,10},{10,6},{6,2},{2,0},{1,5},{5,9},... | collective-permute-start | bytes 589832 | tf_op jit(solution)/shard_map/ppermute | solution.py:258
  18.6 0.7 %grid.12.refs_2_ = f32[8,128,640]{2,1,0:T(8,128)S(1)} custom-call(f32[8,24,256]{2,1,0:T(8,128)S(1)} %collective-permute-done.5.refs_0_, f32[8,24,256]{2,1,0:T(8,128)S(1)} %collective-permute-done.1.refs_1_, f32[8,128,640]{2,1,0:T(8,128)S(1)} %grid.11.refs_2_), custom_call_target="tpu_custom_call", output_to_operand_aliasing={{}: (2, {})} | custom-call | flops 1342177280 | bytes 98304 | tf_op jit(solution)/shard_map/grid/pallas_call | solution.py:169
  19.2 2.8 %collective-permute-done.10.refs_0_ = f32[8,24,256]{2,1,0:T(8,128)S(1)} collective-permute-done((f32[8,24,256]{2,1,0:T(8,128)S(1)}, f32[8,24,256]{2,1,0:T(8,128)S(1)}, u32[]{:S(2)}, u32[]{:S(2)}) %collective-permute-start.10) | collective-permute-done | bytes 196640 | tf_op jit(solution)/shard_map/ppermute | solution.py:258
  22.0 0.0 collective-permute-done.11.refs_1_
  22.1 0.5 %collective-permute-start.12 = (f32[8,24,256]{2,1,0:T(8,128)S(1)}, f32[8,24,256]{2,1,0:T(8,128)S(1)}, u32[]{:S(2)}, u32[]{:S(2)}) collective-permute-start(f32[8,24,256]{2,1,0:T(8,128)S(1)} %collective-permute-done.10.refs_0_), channel_id=1, source_target_pairs={{0,4},{4,8},{8,12},{12,14},{14,10},{10,6},{6,2},{2,0},{1,5},{5,9},... | collective-permute-start | bytes 589832 | tf_op jit(solution)/shard_map/ppermute | solution.py:258
  22.5 1.0 %collective-permute-start.13 = (f32[8,24,256]{2,1,0:T(8,128)S(1)}, f32[8,24,256]{2,1,0:T(8,128)S(1)}, u32[]{:S(2)}, u32[]{:S(2)}) collective-permute-start(f32[8,24,256]{2,1,0:T(8,128)S(1)} %collective-permute-done.11.refs_1_), channel_id=1, source_target_pairs={{4,0},{8,4},{12,8},{14,12},{10,14},{6,10},{2,6},{0,2},{5,1},{9,5},... | collective-permute-start | bytes 589832 | tf_op jit(solution)/shard_map/ppermute | solution.py:258
  23.5 0.8 %grid.13.refs_2_ = f32[8,128,640]{2,1,0:T(8,128)S(1)} custom-call(f32[8,24,256]{2,1,0:T(8,128)S(1)} %collective-permute-done.10.refs_0_, f32[8,24,256]{2,1,0:T(8,128)S(1)} %collective-permute-done.11.refs_1_, f32[8,128,640]{2,1,0:T(8,128)S(1)} %grid.12.refs_2_), custom_call_target="tpu_custom_call", output_to_operand_aliasing={{}: (2, {})} | custom-call | flops 1342177280 | bytes 98304 | tf_op jit(solution)/shard_map/grid/pallas_call | solution.py:169
  24.4 1.9 %collective-permute-done.6.refs_0_ = f32[8,24,256]{2,1,0:T(8,128)S(1)} collective-permute-done((f32[8,24,256]{2,1,0:T(8,128)S(1)}, f32[8,24,256]{2,1,0:T(8,128)S(1)}, u32[]{:S(2)}, u32[]{:S(2)}) %collective-permute-start.6) | collective-permute-done | bytes 196640 | tf_op jit(solution)/shard_map/ppermute | solution.py:258
  26.3 0.2 collective-permute-start.7
  26.5 0.0 collective-permute-done.2.refs_1_
  26.5 1.3 %collective-permute-start.3 = (f32[8,24,256]{2,1,0:T(8,128)S(1)}, f32[8,24,256]{2,1,0:T(8,128)S(1)}, u32[]{:S(2)}, u32[]{:S(2)}) collective-permute-start(f32[8,24,256]{2,1,0:T(8,128)S(1)} %collective-permute-done.2.refs_1_), channel_id=1, source_target_pairs={{4,0},{8,4},{12,8},{14,12},{10,14},{6,10},{2,6},{0,2},{5,1},{9,5},... | collective-permute-start | bytes 589832 | tf_op jit(solution)/shard_map/ppermute | solution.py:258
  27.7 1.1 %grid.14.refs_2_ = f32[8,128,640]{2,1,0:T(8,128)S(1)} custom-call(f32[8,24,256]{2,1,0:T(8,128)S(1)} %collective-permute-done.6.refs_0_, f32[8,24,256]{2,1,0:T(8,128)S(1)} %collective-permute-done.2.refs_1_, f32[8,128,640]{2,1,0:T(8,128)S(1)} %grid.13.refs_2_), custom_call_target="tpu_custom_call", output_to_operand_aliasing={{}: (2, {})} | custom-call | flops 1342177280 | bytes 98304 | tf_op jit(solution)/shard_map/grid/pallas_call | solution.py:169
  28.8 1.7 %collective-permute-done.12.refs_0_ = f32[8,24,256]{2,1,0:T(8,128)S(1)} collective-permute-done((f32[8,24,256]{2,1,0:T(8,128)S(1)}, f32[8,24,256]{2,1,0:T(8,128)S(1)}, u32[]{:S(2)}, u32[]{:S(2)}) %collective-permute-start.12) | collective-permute-done | bytes 196640 | tf_op jit(solution)/shard_map/ppermute | solution.py:258
  30.5 0.0 collective-permute-done.13.refs_1_
  30.5 1.2 %grid.15.refs_1_ = f32[8,128,640]{2,1,0:T(8,128)S(1)} custom-call(f32[8,24,256]{2,1,0:T(8,128)S(1)} %collective-permute-done.12.refs_0_, f32[8,24,256]{2,1,0:T(8,128)S(1)} %collective-permute-done.13.refs_1_, f32[8,128,640]{2,1,0:T(8,128)S(1)} %grid.14.refs_2_), custom_call_target="tpu_custom_call", output_to_operand_aliasing={{}: (2, {})} | custom-call | flops 1342177280 | bytes 98304 | tf_op jit(solution)/shard_map/grid/pallas_call | solution.py:169
  31.7 3.0 %collective-permute-done.7.refs_0_ = f32[8,24,256]{2,1,0:T(8,128)S(1)} collective-permute-done((f32[8,24,256]{2,1,0:T(8,128)S(1)}, f32[8,24,256]{2,1,0:T(8,128)S(1)}, u32[]{:S(2)}, u32[]{:S(2)}) %collective-permute-start.7) | collective-permute-done | bytes 196640 | tf_op jit(solution)/shard_map/ppermute | solution.py:258
  34.7 1.0 %grid.16.refs_1_ = f32[8,128,640]{2,1,0:T(8,128)S(1)} custom-call(f32[8,24,256]{2,1,0:T(8,128)S(1)} %collective-permute-done.7.refs_0_, f32[8,128,640]{2,1,0:T(8,128)S(1)} %grid.15.refs_1_), custom_call_target="tpu_custom_call", output_to_operand_aliasing={{}: (1, {})} | custom-call | flops 671088640 | bytes 49152 | tf_op jit(solution)/shard_map/grid/pallas_call | solution.py:169
  35.7 0.0 copy-start
  35.7 0.0 collective-permute-done.3.refs_0_
  35.7 0.8 %grid.17 = (f32[8,128,640]{2,1,0:T(8,128)S(1)}, f32[16,128]{1,0:T(8,128)S(1)}) custom-call(f32[8,24,256]{2,1,0:T(8,128)S(1)} %collective-permute-done.3.refs_0_, f32[8,128,640]{2,1,0:T(8,128)S(1)} %grid.16.refs_1_), custom_call_target="tpu_custom_call", output_to_operand_aliasing={{0}: (1, {})} | custom-call | flops 671088640 | bytes 49152 | tf_op jit(solution)/shard_map/grid/pallas_call | solution.py:169
  36.6 1.9 %collective-permute-start.14 = (f32[16,128]{1,0:T(8,128)S(1)}, f32[16,128]{1,0:T(8,128)S(1)}, u32[]{:S(2)}, u32[]{:S(2)}) collective-permute-start(f32[16,128]{1,0:T(8,128)S(1)} %get-tuple-element.30.mine_ref), channel_id=1, source_target_pairs={{0,1},{1,0},{2,3},{3,2},{4,5},{5,4},{6,7},{7,6},{8,9},{9,8},{10,11... | collective-permute-start | bytes 24584 | tf_op jit(solution)/shard_map/ppermute | solution.py:313
  38.4 0.9 %dynamic-slice_bitcast_fusion.row_ref = bf16[128,512]{1,0:T(8,128)(2,1)S(1)} fusion(bf16[8,128,512]{2,1,0:T(8,128)(2,1)} %constant.16.clone, s32[]{:T(128)S(6)} %select_n.4), kind=kLoop, calls=%fused_computation | loop fusion | bytes 262148 | tf_op jit(solution)/shard_map/jit(dynamic_index_in_dim)/squeeze | solution.py:315
  39.3 0.0 collective-permute-done.14.other_ref
  39.4 0.0 copy-done
  39.4 1.6 %image.1 = f32[2,2,2,32,256]{4,3,2,1,0:T(8,128)} custom-call(f32[8,128,640]{2,1,0:T(8,128)S(1)} %get-tuple-element.29.acc_ref, f32[16,128]{1,0:T(8,128)S(1)} %get-tuple-element.30.mine_ref, f32[16,128]{1,0:T(8,128)S(1)} %collective-permute-done.14.other_ref, bf16[128,512]{1,0:T(8,128)(2,1)S(1)} %dynamic-slice_bitcast_fusion.row_ref, ...), custom_call_target="tpu_custom_call" | custom-call | tf_op jit(solution)/shard_map/image/pallas_call | solution.py:222
Async XLA Ops:
  1.9 6.8 %collective-permute-start = (f32[8,24,256]{2,1,0:T(8,128)S(1)}, f32[8,24,256]{2,1,0:T(8,128)S(1)}, u32[]{:S(2)}, u32[]{:S(2)}) collective-permute-start(f32[8,24,256]{2,1,0:T(8,128)S(1)} %get-tuple-element.18.refs_1_), channel_id=1, source_target_pairs={{4,0},{8,4},{12,8},{14,12},{10,14},{6,10},{2,6},{0,2},{5,1},{9,5},... | collective-permute-start | bytes 589832 | tf_op jit(solution)/shard_map/ppermute | solution.py:258
  4.0 5.8 %collective-permute-start.4 = (f32[8,24,256]{2,1,0:T(8,128)S(1)}, f32[8,24,256]{2,1,0:T(8,128)S(1)}, u32[]{:S(2)}, u32[]{:S(2)}) collective-permute-start(f32[8,24,256]{2,1,0:T(8,128)S(1)} %get-tuple-element.19.refs_0_), channel_id=1, source_target_pairs={{0,4},{4,8},{8,12},{12,14},{14,10},{10,6},{6,2},{2,0},{1,5},{5,9},... | collective-permute-start | bytes 589832 | tf_op jit(solution)/shard_map/ppermute | solution.py:258
  4.1 9.5 %collective-permute-start.8 = (f32[8,24,256]{2,1,0:T(8,128)S(1)}, f32[8,24,256]{2,1,0:T(8,128)S(1)}, u32[]{:S(2)}, u32[]{:S(2)}) collective-permute-start(f32[8,24,256]{2,1,0:T(8,128)S(1)} %get-tuple-element.18.refs_1_), channel_id=1, source_target_pairs={{0,4},{4,8},{8,12},{12,14},{14,10},{10,6},{6,2},{2,0},{1,5},{5,9},... | collective-permute-start | bytes 589832 | tf_op jit(solution)/shard_map/ppermute | solution.py:258
  5.5 8.1 %collective-permute-start.9 = (f32[8,24,256]{2,1,0:T(8,128)S(1)}, f32[8,24,256]{2,1,0:T(8,128)S(1)}, u32[]{:S(2)}, u32[]{:S(2)}) collective-permute-start(f32[8,24,256]{2,1,0:T(8,128)S(1)} %get-tuple-element.19.refs_0_), channel_id=1, source_target_pairs={{4,0},{8,4},{12,8},{14,12},{10,14},{6,10},{2,6},{0,2},{5,1},{9,5},... | collective-permute-start | bytes 589832 | tf_op jit(solution)/shard_map/ppermute | solution.py:258
  8.7 8.4 %collective-permute-start.1 = (f32[8,24,256]{2,1,0:T(8,128)S(1)}, f32[8,24,256]{2,1,0:T(8,128)S(1)}, u32[]{:S(2)}, u32[]{:S(2)}) collective-permute-start(f32[8,24,256]{2,1,0:T(8,128)S(1)} %collective-permute-done.refs_1_), channel_id=1, source_target_pairs={{4,0},{8,4},{12,8},{14,12},{10,14},{6,10},{2,6},{0,2},{5,1},{9,5},... | collective-permute-start | bytes 589832 | tf_op jit(solution)/shard_map/ppermute | solution.py:258
  9.7 8.4 %collective-permute-start.5 = (f32[8,24,256]{2,1,0:T(8,128)S(1)}, f32[8,24,256]{2,1,0:T(8,128)S(1)}, u32[]{:S(2)}, u32[]{:S(2)}) collective-permute-start(f32[8,24,256]{2,1,0:T(8,128)S(1)} %collective-permute-done.4.refs_0_), channel_id=1, source_target_pairs={{0,4},{4,8},{8,12},{12,14},{14,10},{10,6},{6,2},{2,0},{1,5},{5,9},... | collective-permute-start | bytes 589832 | tf_op jit(solution)/shard_map/ppermute | solution.py:258
  13.6 8.4 %collective-permute-start.10 = (f32[8,24,256]{2,1,0:T(8,128)S(1)}, f32[8,24,256]{2,1,0:T(8,128)S(1)}, u32[]{:S(2)}, u32[]{:S(2)}) collective-permute-start(f32[8,24,256]{2,1,0:T(8,128)S(1)} %collective-permute-done.8.refs_0_), channel_id=1, source_target_pairs={{0,4},{4,8},{8,12},{12,14},{14,10},{10,6},{6,2},{2,0},{1,5},{5,9},... | collective-permute-start | bytes 589832 | tf_op jit(solution)/shard_map/ppermute | solution.py:258
  14.1 8.0 %collective-permute-start.11 = (f32[8,24,256]{2,1,0:T(8,128)S(1)}, f32[8,24,256]{2,1,0:T(8,128)S(1)}, u32[]{:S(2)}, u32[]{:S(2)}) collective-permute-start(f32[8,24,256]{2,1,0:T(8,128)S(1)} %collective-permute-done.9.refs_1_), channel_id=1, source_target_pairs={{4,0},{8,4},{12,8},{14,12},{10,14},{6,10},{2,6},{0,2},{5,1},{9,5},... | collective-permute-start | bytes 589832 | tf_op jit(solution)/shard_map/ppermute | solution.py:258
  17.1 9.4 %collective-permute-start.2 = (f32[8,24,256]{2,1,0:T(8,128)S(1)}, f32[8,24,256]{2,1,0:T(8,128)S(1)}, u32[]{:S(2)}, u32[]{:S(2)}) collective-permute-start(f32[8,24,256]{2,1,0:T(8,128)S(1)} %collective-permute-done.1.refs_1_), channel_id=1, source_target_pairs={{4,0},{8,4},{12,8},{14,12},{10,14},{6,10},{2,6},{0,2},{5,1},{9,5},... | collective-permute-start | bytes 589832 | tf_op jit(solution)/shard_map/ppermute | solution.py:258
  18.2 8.1 %collective-permute-start.6 = (f32[8,24,256]{2,1,0:T(8,128)S(1)}, f32[8,24,256]{2,1,0:T(8,128)S(1)}, u32[]{:S(2)}, u32[]{:S(2)}) collective-permute-start(f32[8,24,256]{2,1,0:T(8,128)S(1)} %collective-permute-done.5.refs_0_), channel_id=1, source_target_pairs={{0,4},{4,8},{8,12},{12,14},{14,10},{10,6},{6,2},{2,0},{1,5},{5,9},... | collective-permute-start | bytes 589832 | tf_op jit(solution)/shard_map/ppermute | solution.py:258
  22.1 8.4 %collective-permute-start.12 = (f32[8,24,256]{2,1,0:T(8,128)S(1)}, f32[8,24,256]{2,1,0:T(8,128)S(1)}, u32[]{:S(2)}, u32[]{:S(2)}) collective-permute-start(f32[8,24,256]{2,1,0:T(8,128)S(1)} %collective-permute-done.10.refs_0_), channel_id=1, source_target_pairs={{0,4},{4,8},{8,12},{12,14},{14,10},{10,6},{6,2},{2,0},{1,5},{5,9},... | collective-permute-start | bytes 589832 | tf_op jit(solution)/shard_map/ppermute | solution.py:258
  22.5 8.0 %collective-permute-start.13 = (f32[8,24,256]{2,1,0:T(8,128)S(1)}, f32[8,24,256]{2,1,0:T(8,128)S(1)}, u32[]{:S(2)}, u32[]{:S(2)}) collective-permute-start(f32[8,24,256]{2,1,0:T(8,128)S(1)} %collective-permute-done.11.refs_1_), channel_id=1, source_target_pairs={{4,0},{8,4},{12,8},{14,12},{10,14},{6,10},{2,6},{0,2},{5,1},{9,5},... | collective-permute-start | bytes 589832 | tf_op jit(solution)/shard_map/ppermute | solution.py:258
  26.3 8.4 %collective-permute-start.7 = (f32[8,24,256]{2,1,0:T(8,128)S(1)}, f32[8,24,256]{2,1,0:T(8,128)S(1)}, u32[]{:S(2)}, u32[]{:S(2)}) collective-permute-start(f32[8,24,256]{2,1,0:T(8,128)S(1)} %collective-permute-done.6.refs_0_), channel_id=1, source_target_pairs={{0,4},{4,8},{8,12},{12,14},{14,10},{10,6},{6,2},{2,0},{1,5},{5,9},... | collective-permute-start | bytes 589832 | tf_op jit(solution)/shard_map/ppermute | solution.py:258
  26.5 9.3 %collective-permute-start.3 = (f32[8,24,256]{2,1,0:T(8,128)S(1)}, f32[8,24,256]{2,1,0:T(8,128)S(1)}, u32[]{:S(2)}, u32[]{:S(2)}) collective-permute-start(f32[8,24,256]{2,1,0:T(8,128)S(1)} %collective-permute-done.2.refs_1_), channel_id=1, source_target_pairs={{4,0},{8,4},{12,8},{14,12},{10,14},{6,10},{2,6},{0,2},{5,1},{9,5},... | collective-permute-start | bytes 589832 | tf_op jit(solution)/shard_map/ppermute | solution.py:258
  35.7 3.7 %copy-start = (bf16[256,1024]{1,0:T(8,128)(2,1)S(1)}, bf16[256,1024]{1,0:T(8,128)(2,1)}, u32[]{:S(2)}) copy-start(bf16[256,1024]{1,0:T(8,128)(2,1)} %constant.17.clone.col_ref) | copy-start | bytes 1572868
  36.6 2.8 %collective-permute-start.14 = (f32[16,128]{1,0:T(8,128)S(1)}, f32[16,128]{1,0:T(8,128)S(1)}, u32[]{:S(2)}, u32[]{:S(2)}) collective-permute-start(f32[16,128]{1,0:T(8,128)S(1)} %get-tuple-element.30.mine_ref), channel_id=1, source_target_pairs={{0,1},{1,0},{2,3},{3,2},{4,5},{5,4},{6,7},{7,6},{8,9},{9,8},{10,11... | collective-permute-start | bytes 24584 | tf_op jit(solution)/shard_map/ppermute | solution.py:313
where the time goes:
time: 41 us
  Pallas kernels  13.3 us (32%)
  waiting for transfers between devices  13.1 us (32%)
  starting transfers between devices  12.9 us (31%)
  local copies, waits for them, and re-layouts  0.92 us (2%)
  between operations  0.77 us (2%)
    ppermute x14, waiting for transfers between devices, both_ways(): return [lax.ppermute(pair[0], 'tm', up), lax.ppermute(pair[1], 'tm', down)]  13.1 us
    ppermute x14, starting transfers between devices, both_ways(): return [lax.ppermute(pair[0], 'tm', up), lax.ppermute(pair[1], 'tm', down)]  11 us
    pallas_call x9, Pallas kernels, add_blocks(): pl.pallas_call(lambda *refs: grid_kernel(n, first, last, *refs), out_shap...  10.5 us
    ppermute x1, starting transfers between devices, body(): lax.ppermute(mine, 'tile', [(i, n_tile - 1 - i) for i in range(n_tile)])  1.87 us
    pallas_call x1, Pallas kernels, make_image(): pl.pallas_call(image_kernel, out_shape=jax.ShapeDtypeStruct((POLS, 2, NT_...  1.61 us
    pallas_call x1, Pallas kernels, pack(): pl.pallas_call(lambda *refs: pack_kernel(pieces, *refs), out_shape=[jax.S...  1.2 us
    squeeze x1, local copies, waits for them, and re-layouts, body(): lax.dynamic_index_in_dim(jnp.asarray(row_tables), lax.axis_index('tm'), 0...  0.91 us
  transfers between devices with their start and end apart: 15, of which 7 were waited for; matrix products, arithmetic and copies ran while one was open for 2% of the time, Pallas kernels for 24%

commit v1 on v0

--- a/solution.py
+++ b/solution.py
@@ -249,13 +249,17 @@
     return np.stack(rows), np_parts(np.concatenate([cosine, sine], axis=1) / G, 1)
 
 
-def by_gather(packed, n_tm):
+def by_gather(packed, n_tm, n_tile):
     order = list(range(0, n_tm, 2)) + list(range(1, n_tm, 2))[::-1]
-    up = [(order[i], order[(i + 1) % n_tm]) for i in range(n_tm)]
-    down = [(b, a) for a, b in up]
+    ways = [[], []]
+    for i in range(n_tm):
+        for tile in range(n_tile):
+            here, there = (n_tile * order[k] + tile for k in (i, (i + 1) % n_tm))
+            ways[tile % 2].append((here, there))
+            ways[1 - tile % 2].append((there, here))
 
     def both_ways(pair):
-        return [lax.ppermute(pair[0], "tm", up), lax.ppermute(pair[1], "tm", down)]
+        return [lax.ppermute(a, ("tm", "tile"), way) for a, way in zip(pair, ways)]
 
     leading = both_ways(packed)
     trailing = both_ways(packed[::-1])
@@ -308,8 +312,8 @@
     if n_tm > 8:
         cosine, sine = dft_tables()
         return rest_by_rows(add_blocks(None, packed), jnp.asarray(cosine), jnp.asarray(sine))
-    acc, mine = by_gather(packed, n_tm)
     n_tile = lax.axis_size("tile")
+    acc, mine = by_gather(packed, n_tm, n_tile)
     other = lax.ppermute(mine, "tile", [(i, n_tile - 1 - i) for i in range(n_tile)])
     row_tables, col_table = image_tables(n_tm)
     row_table = lax.dynamic_index_in_dim(jnp.asarray(row_tables), lax.axis_index("tm"), 0, keepdims=False)

time: 41 us -> 40.6 us (level)
  waiting for transfers between devices: 13.1 us -> 8.61 us
  starting transfers between devices: 12.9 us -> 16.8 us
    ppermute x14, waiting for transfers between devices: 13.1 us -> 8.61 us  [both_ways(): return [lax.ppermute(a, ('tm', 'tile'), way) for a, way in zip(pair, ways)]]
    ppermute x1, starting transfers between devices: 1.87 us -> 3.83 us  [body(): lax.ppermute(mine, 'tile', [(i, n_tile - 1 - i) for i in range(n_tile)])]
    ppermute x14, starting transfers between devices: 11 us -> 13 us  [both_ways(): return [lax.ppermute(a, ('tm', 'tile'), way) for a, way in zip(pair, ways)]]
  transfers between devices with their start and end apart: 15 -> 15, of which waited for: 7 -> 7; matrix products, arithmetic and copies ran while one was open for 2% -> 2% of each run, Pallas kernels for 24% -> 25%
where the time goes in v1:
time: 40.6 us; the launch traced here: 40.3 us
  starting transfers between devices  16.8 us (41%)
  Pallas kernels  13.1 us (32%)
  waiting for transfers between devices  8.61 us (21%)
  local copies, waits for them, and re-layouts  0.92 us (2%)
  between operations  0.79 us (2%)
    ppermute x14, starting transfers between devices, both_ways(): return [lax.ppermute(a, ('tm', 'tile'), way) for a, way in zip(pair, ways)]  13 us
    pallas_call x9, Pallas kernels, add_blocks(): pl.pallas_call(lambda *refs: grid_kernel(n, first, last, *refs), out_shap...  10.3 us
    ppermute x14, waiting for transfers between devices, both_ways(): return [lax.ppermute(a, ('tm', 'tile'), way) for a, way in zip(pair, ways)]  8.61 us
    ppermute x1, starting transfers between devices, body(): lax.ppermute(mine, 'tile', [(i, n_tile - 1 - i) for i in range(n_tile)])  3.83 us
    pallas_call x1, Pallas kernels, make_image(): pl.pallas_call(image_kernel, out_shape=jax.ShapeDtypeStruct((POLS, 2, NT_...  1.6 us
    pallas_call x1, Pallas kernels, pack(): pl.pallas_call(lambda *refs: pack_kernel(pieces, *refs), out_shape=[jax.S...  1.2 us
    squeeze x1, local copies, waits for them, and re-layouts, body(): lax.dynamic_index_in_dim(jnp.asarray(row_tables), lax.axis_index('tm'), 0...  0.91 us
  transfers between devices with their start and end apart: 15, of which 7 were waited for; matrix products, arithmetic and copies ran while one was open for 2% of the time, Pallas kernels for 25%

profile of v1, /device:TPU:1, one launch (start us, length us, event | category | flops | bytes accessed | tf_op | source)
XLA Modules:
  0.0 40.3 jit_solution(3730331353810851938)
XLA Ops:
  0.7 1.2 %pack.1 = (f32[8,24,256]{2,1,0:T(8,128)S(1)}, f32[8,24,256]{2,1,0:T(8,128)S(1)}) custom-call(f32[16,4,256]{2,1,0:T(4,128)} %bitcast.7, f32[16,256]{1,0:T(8,128)} %bitcast.9, f32[16,2,8,256]{3,2,1,0:T(8,128)} %bitcast.6, s32[16,2,256]{2,1,0:T(2,128)} %bitcast.8, s32[1,16]{1,0:T(1,128)} %refs_4_.1, s32[1,1]{1,0:T(1,128)S(6)} %copy.25.refs_5_), custom_call_target="tpu_custom_call" | custom-call | tf_op jit(solution)/shard_map/pack/pallas_call | solution.py:78
  1.9 2.2 %collective-permute-start = (f32[8,24,256]{2,1,0:T(8,128)S(1)}, f32[8,24,256]{2,1,0:T(8,128)S(1)}, u32[]{:S(2)}, u32[]{:S(2)}) collective-permute-start(f32[8,24,256]{2,1,0:T(8,128)S(1)} %get-tuple-element.18.refs_1_), channel_id=1, source_target_pairs={{4,0},{1,5},{8,4},{5,9},{12,8},{9,13},{14,12},{13,15},{10,14},{15,... | collective-permute-start | bytes 589832 | tf_op jit(solution)/shard_map/ppermute | solution.py:262
  4.0 0.0 collective-permute-start.4
  4.0 1.4 %collective-permute-start.8 = (f32[8,24,256]{2,1,0:T(8,128)S(1)}, f32[8,24,256]{2,1,0:T(8,128)S(1)}, u32[]{:S(2)}, u32[]{:S(2)}) collective-permute-start(f32[8,24,256]{2,1,0:T(8,128)S(1)} %get-tuple-element.18.refs_1_), channel_id=1, source_target_pairs={{0,4},{5,1},{4,8},{9,5},{8,12},{13,9},{12,14},{15,13},{14,10},{11,... | collective-permute-start | bytes 589832 | tf_op jit(solution)/shard_map/ppermute | solution.py:262
  5.4 0.1 collective-permute-start.9
  5.5 0.8 %grid.9.refs_2_ = f32[8,128,640]{2,1,0:T(8,128)S(1)} custom-call(f32[8,24,256]{2,1,0:T(8,128)S(1)} %get-tuple-element.19.refs_0_, f32[8,24,256]{2,1,0:T(8,128)S(1)} %get-tuple-element.18.refs_1_), custom_call_target="tpu_custom_call" | custom-call | flops 1342177280 | bytes 98304 | tf_op jit(solution)/shard_map/grid/pallas_call | solution.py:169
  6.4 1.1 %collective-permute-done.refs_1_ = f32[8,24,256]{2,1,0:T(8,128)S(1)} collective-permute-done((f32[8,24,256]{2,1,0:T(8,128)S(1)}, f32[8,24,256]{2,1,0:T(8,128)S(1)}, u32[]{:S(2)}, u32[]{:S(2)}) %collective-permute-start) | collective-permute-done | bytes 196640 | tf_op jit(solution)/shard_map/ppermute | solution.py:262
  7.5 2.2 %collective-permute-start.1 = (f32[8,24,256]{2,1,0:T(8,128)S(1)}, f32[8,24,256]{2,1,0:T(8,128)S(1)}, u32[]{:S(2)}, u32[]{:S(2)}) collective-permute-start(f32[8,24,256]{2,1,0:T(8,128)S(1)} %collective-permute-done.refs_1_), channel_id=1, source_target_pairs={{4,0},{1,5},{8,4},{5,9},{12,8},{9,13},{14,12},{13,15},{10,14},{15,... | collective-permute-start | bytes 589832 | tf_op jit(solution)/shard_map/ppermute | solution.py:262
  9.7 0.7 %collective-permute-done.4.refs_0_ = f32[8,24,256]{2,1,0:T(8,128)S(1)} collective-permute-done((f32[8,24,256]{2,1,0:T(8,128)S(1)}, f32[8,24,256]{2,1,0:T(8,128)S(1)}, u32[]{:S(2)}, u32[]{:S(2)}) %collective-permute-start.4) | collective-permute-done | bytes 196640 | tf_op jit(solution)/shard_map/ppermute | solution.py:262
  10.5 0.0 collective-permute-start.5
  10.5 1.6 %grid.10.refs_2_ = f32[8,128,640]{2,1,0:T(8,128)S(1)} custom-call(f32[8,24,256]{2,1,0:T(8,128)S(1)} %collective-permute-done.4.refs_0_, f32[8,24,256]{2,1,0:T(8,128)S(1)} %collective-permute-done.refs_1_, f32[8,128,640]{2,1,0:T(8,128)S(1)} %grid.9.refs_2_), custom_call_target="tpu_custom_call", output_to_operand_aliasing={{}: (2, {})} | custom-call | flops 1342177280 | bytes 98304 | tf_op jit(solution)/shard_map/grid/pallas_call | solution.py:169
  12.1 2.6 %collective-permute-done.8.refs_0_ = f32[8,24,256]{2,1,0:T(8,128)S(1)} collective-permute-done((f32[8,24,256]{2,1,0:T(8,128)S(1)}, f32[8,24,256]{2,1,0:T(8,128)S(1)}, u32[]{:S(2)}, u32[]{:S(2)}) %collective-permute-start.8) | collective-permute-done | bytes 196640 | tf_op jit(solution)/shard_map/ppermute | solution.py:262
  14.7 0.0 collective-permute-done.9.refs_1_
  14.7 0.0 collective-permute-start.10
  14.7 1.8 %collective-permute-start.11 = (f32[8,24,256]{2,1,0:T(8,128)S(1)}, f32[8,24,256]{2,1,0:T(8,128)S(1)}, u32[]{:S(2)}, u32[]{:S(2)}) collective-permute-start(f32[8,24,256]{2,1,0:T(8,128)S(1)} %collective-permute-done.9.refs_1_), channel_id=1, source_target_pairs={{4,0},{1,5},{8,4},{5,9},{12,8},{9,13},{14,12},{13,15},{10,14},{15,... | collective-permute-start | bytes 589832 | tf_op jit(solution)/shard_map/ppermute | solution.py:262
  16.5 1.1 %grid.11.refs_2_ = f32[8,128,640]{2,1,0:T(8,128)S(1)} custom-call(f32[8,24,256]{2,1,0:T(8,128)S(1)} %collective-permute-done.8.refs_0_, f32[8,24,256]{2,1,0:T(8,128)S(1)} %collective-permute-done.9.refs_1_, f32[8,128,640]{2,1,0:T(8,128)S(1)} %grid.10.refs_2_), custom_call_target="tpu_custom_call", output_to_operand_aliasing={{}: (2, {})} | custom-call | flops 1342177280 | bytes 98304 | tf_op jit(solution)/shard_map/grid/pallas_call | solution.py:169
  17.5 0.0 collective-permute-done.1.refs_1_
  17.6 2.1 %collective-permute-start.2 = (f32[8,24,256]{2,1,0:T(8,128)S(1)}, f32[8,24,256]{2,1,0:T(8,128)S(1)}, u32[]{:S(2)}, u32[]{:S(2)}) collective-permute-start(f32[8,24,256]{2,1,0:T(8,128)S(1)} %collective-permute-done.1.refs_1_), channel_id=1, source_target_pairs={{4,0},{1,5},{8,4},{5,9},{12,8},{9,13},{14,12},{13,15},{10,14},{15,... | collective-permute-start | bytes 589832 | tf_op jit(solution)/shard_map/ppermute | solution.py:262
  19.6 0.0 collective-permute-done.5.refs_0_
  19.6 0.0 collective-permute-start.6
  19.6 1.1 %grid.12.refs_2_ = f32[8,128,640]{2,1,0:T(8,128)S(1)} custom-call(f32[8,24,256]{2,1,0:T(8,128)S(1)} %collective-permute-done.5.refs_0_, f32[8,24,256]{2,1,0:T(8,128)S(1)} %collective-permute-done.1.refs_1_, f32[8,128,640]{2,1,0:T(8,128)S(1)} %grid.11.refs_2_), custom_call_target="tpu_custom_call", output_to_operand_aliasing={{}: (2, {})} | custom-call | flops 1342177280 | bytes 98304 | tf_op jit(solution)/shard_map/grid/pallas_call | solution.py:169
  20.7 0.8 %collective-permute-done.10.refs_0_ = f32[8,24,256]{2,1,0:T(8,128)S(1)} collective-permute-done((f32[8,24,256]{2,1,0:T(8,128)S(1)}, f32[8,24,256]{2,1,0:T(8,128)S(1)}, u32[]{:S(2)}, u32[]{:S(2)}) %collective-permute-start.10) | collective-permute-done | bytes 196640 | tf_op jit(solution)/shard_map/ppermute | solution.py:262
  21.5 0.0 collective-permute-done.11.refs_1_
  21.5 1.1 %collective-permute-start.12 = (f32[8,24,256]{2,1,0:T(8,128)S(1)}, f32[8,24,256]{2,1,0:T(8,128)S(1)}, u32[]{:S(2)}, u32[]{:S(2)}) collective-permute-start(f32[8,24,256]{2,1,0:T(8,128)S(1)} %collective-permute-done.10.refs_0_), channel_id=1, source_target_pairs={{0,4},{5,1},{4,8},{9,5},{8,12},{13,9},{12,14},{15,13},{14,10},{11,... | collective-permute-start | bytes 589832 | tf_op jit(solution)/shard_map/ppermute | solution.py:262
  22.6 0.7 %collective-permute-start.13 = (f32[8,24,256]{2,1,0:T(8,128)S(1)}, f32[8,24,256]{2,1,0:T(8,128)S(1)}, u32[]{:S(2)}, u32[]{:S(2)}) collective-permute-start(f32[8,24,256]{2,1,0:T(8,128)S(1)} %collective-permute-done.11.refs_1_), channel_id=1, source_target_pairs={{4,0},{1,5},{8,4},{5,9},{12,8},{9,13},{14,12},{13,15},{10,14},{15,... | collective-permute-start | bytes 589832 | tf_op jit(solution)/shard_map/ppermute | solution.py:262
  23.2 2.2 %grid.13.refs_2_ = f32[8,128,640]{2,1,0:T(8,128)S(1)} custom-call(f32[8,24,256]{2,1,0:T(8,128)S(1)} %collective-permute-done.10.refs_0_, f32[8,24,256]{2,1,0:T(8,128)S(1)} %collective-permute-done.11.refs_1_, f32[8,128,640]{2,1,0:T(8,128)S(1)} %grid.12.refs_2_), custom_call_target="tpu_custom_call", output_to_operand_aliasing={{}: (2, {})} | custom-call | flops 1342177280 | bytes 98304 | tf_op jit(solution)/shard_map/grid/pallas_call | solution.py:169
  25.4 1.2 %collective-permute-done.6.refs_0_ = f32[8,24,256]{2,1,0:T(8,128)S(1)} collective-permute-done((f32[8,24,256]{2,1,0:T(8,128)S(1)}, f32[8,24,256]{2,1,0:T(8,128)S(1)}, u32[]{:S(2)}, u32[]{:S(2)}) %collective-permute-start.6) | collective-permute-done | bytes 196640 | tf_op jit(solution)/shard_map/ppermute | solution.py:262
  26.6 0.0 collective-permute-start.7
  26.6 0.0 collective-permute-done.2.refs_1_
  26.6 1.5 %collective-permute-start.3 = (f32[8,24,256]{2,1,0:T(8,128)S(1)}, f32[8,24,256]{2,1,0:T(8,128)S(1)}, u32[]{:S(2)}, u32[]{:S(2)}) collective-permute-start(f32[8,24,256]{2,1,0:T(8,128)S(1)} %collective-permute-done.2.refs_1_), channel_id=1, source_target_pairs={{4,0},{1,5},{8,4},{5,9},{12,8},{9,13},{14,12},{13,15},{10,14},{15,... | collective-permute-start | bytes 589832 | tf_op jit(solution)/shard_map/ppermute | solution.py:262
  28.1 1.6 %grid.14.refs_2_ = f32[8,128,640]{2,1,0:T(8,128)S(1)} custom-call(f32[8,24,256]{2,1,0:T(8,128)S(1)} %collective-permute-done.6.refs_0_, f32[8,24,256]{2,1,0:T(8,128)S(1)} %collective-permute-done.2.refs_1_, f32[8,128,640]{2,1,0:T(8,128)S(1)} %grid.13.refs_2_), custom_call_target="tpu_custom_call", output_to_operand_aliasing={{}: (2, {})} | custom-call | flops 1342177280 | bytes 98304 | tf_op jit(solution)/shard_map/grid/pallas_call | solution.py:169
  29.7 0.0 collective-permute-done.12.refs_0_
  29.7 0.0 collective-permute-done.13.refs_1_
  29.7 1.1 %grid.15.refs_1_ = f32[8,128,640]{2,1,0:T(8,128)S(1)} custom-call(f32[8,24,256]{2,1,0:T(8,128)S(1)} %collective-permute-done.12.refs_0_, f32[8,24,256]{2,1,0:T(8,128)S(1)} %collective-permute-done.13.refs_1_, f32[8,128,640]{2,1,0:T(8,128)S(1)} %grid.14.refs_2_), custom_call_target="tpu_custom_call", output_to_operand_aliasing={{}: (2, {})} | custom-call | flops 1342177280 | bytes 98304 | tf_op jit(solution)/shard_map/grid/pallas_call | solution.py:169
  30.8 2.0 %collective-permute-done.7.refs_0_ = f32[8,24,256]{2,1,0:T(8,128)S(1)} collective-permute-done((f32[8,24,256]{2,1,0:T(8,128)S(1)}, f32[8,24,256]{2,1,0:T(8,128)S(1)}, u32[]{:S(2)}, u32[]{:S(2)}) %collective-permute-start.7) | collective-permute-done | bytes 196640 | tf_op jit(solution)/shard_map/ppermute | solution.py:262
  32.9 0.6 %grid.16.refs_1_ = f32[8,128,640]{2,1,0:T(8,128)S(1)} custom-call(f32[8,24,256]{2,1,0:T(8,128)S(1)} %collective-permute-done.7.refs_0_, f32[8,128,640]{2,1,0:T(8,128)S(1)} %grid.15.refs_1_), custom_call_target="tpu_custom_call", output_to_operand_aliasing={{}: (1, {})} | custom-call | flops 671088640 | bytes 49152 | tf_op jit(solution)/shard_map/grid/pallas_call | solution.py:169
  33.5 0.0 copy-start
  33.5 0.2 collective-permute-done.3.refs_0_
  33.6 0.3 grid.17
  33.9 3.8 %collective-permute-start.14 = (f32[16,128]{1,0:T(8,128)S(1)}, f32[16,128]{1,0:T(8,128)S(1)}, u32[]{:S(2)}, u32[]{:S(2)}) collective-permute-start(f32[16,128]{1,0:T(8,128)S(1)} %get-tuple-element.30.mine_ref), channel_id=1, source_target_pairs={{0,1},{1,0},{2,3},{3,2},{4,5},{5,4},{6,7},{7,6},{8,9},{9,8},{10,11... | collective-permute-start | bytes 24584 | tf_op jit(solution)/shard_map/ppermute | solution.py:317
  37.7 0.9 %dynamic-slice_bitcast_fusion.row_ref = bf16[128,512]{1,0:T(8,128)(2,1)S(1)} fusion(bf16[8,128,512]{2,1,0:T(8,128)(2,1)} %constant.16.clone, s32[]{:T(128)S(6)} %select_n.4), kind=kLoop, calls=%fused_computation | loop fusion | bytes 262148 | tf_op jit(solution)/shard_map/jit(dynamic_index_in_dim)/squeeze | solution.py:319
  38.7 0.0 collective-permute-done.14.other_ref
  38.7 0.0 copy-done
  38.7 1.6 %image.1 = f32[2,2,2,32,256]{4,3,2,1,0:T(8,128)} custom-call(f32[8,128,640]{2,1,0:T(8,128)S(1)} %get-tuple-element.29.acc_ref, f32[16,128]{1,0:T(8,128)S(1)} %get-tuple-element.30.mine_ref, f32[16,128]{1,0:T(8,128)S(1)} %collective-permute-done.14.other_ref, bf16[128,512]{1,0:T(8,128)(2,1)S(1)} %dynamic-slice_bitcast_fusion.row_ref, ...), custom_call_target="tpu_custom_call" | custom-call | tf_op jit(solution)/shard_map/image/pallas_call | solution.py:222
Async XLA Ops:
  1.9 5.7 %collective-permute-start = (f32[8,24,256]{2,1,0:T(8,128)S(1)}, f32[8,24,256]{2,1,0:T(8,128)S(1)}, u32[]{:S(2)}, u32[]{:S(2)}) collective-permute-start(f32[8,24,256]{2,1,0:T(8,128)S(1)} %get-tuple-element.18.refs_1_), channel_id=1, source_target_pairs={{4,0},{1,5},{8,4},{5,9},{12,8},{9,13},{14,12},{13,15},{10,14},{15,... | collective-permute-start | bytes 589832 | tf_op jit(solution)/shard_map/ppermute | solution.py:262
  4.0 6.4 %collective-permute-start.4 = (f32[8,24,256]{2,1,0:T(8,128)S(1)}, f32[8,24,256]{2,1,0:T(8,128)S(1)}, u32[]{:S(2)}, u32[]{:S(2)}) collective-permute-start(f32[8,24,256]{2,1,0:T(8,128)S(1)} %get-tuple-element.19.refs_0_), channel_id=1, source_target_pairs={{0,4},{5,1},{4,8},{9,5},{8,12},{13,9},{12,14},{15,13},{14,10},{11,... | collective-permute-start | bytes 589832 | tf_op jit(solution)/shard_map/ppermute | solution.py:262
  4.0 10.6 %collective-permute-start.8 = (f32[8,24,256]{2,1,0:T(8,128)S(1)}, f32[8,24,256]{2,1,0:T(8,128)S(1)}, u32[]{:S(2)}, u32[]{:S(2)}) collective-permute-start(f32[8,24,256]{2,1,0:T(8,128)S(1)} %get-tuple-element.18.refs_1_), channel_id=1, source_target_pairs={{0,4},{5,1},{4,8},{9,5},{8,12},{13,9},{12,14},{15,13},{14,10},{11,... | collective-permute-start | bytes 589832 | tf_op jit(solution)/shard_map/ppermute | solution.py:262
  5.4 9.3 %collective-permute-start.9 = (f32[8,24,256]{2,1,0:T(8,128)S(1)}, f32[8,24,256]{2,1,0:T(8,128)S(1)}, u32[]{:S(2)}, u32[]{:S(2)}) collective-permute-start(f32[8,24,256]{2,1,0:T(8,128)S(1)} %get-tuple-element.19.refs_0_), channel_id=1, source_target_pairs={{4,0},{1,5},{8,4},{5,9},{12,8},{9,13},{14,12},{13,15},{10,14},{15,... | collective-permute-start | bytes 589832 | tf_op jit(solution)/shard_map/ppermute | solution.py:262
  7.5 10.0 %collective-permute-start.1 = (f32[8,24,256]{2,1,0:T(8,128)S(1)}, f32[8,24,256]{2,1,0:T(8,128)S(1)}, u32[]{:S(2)}, u32[]{:S(2)}) collective-permute-start(f32[8,24,256]{2,1,0:T(8,128)S(1)} %collective-permute-done.refs_1_), channel_id=1, source_target_pairs={{4,0},{1,5},{8,4},{5,9},{12,8},{9,13},{14,12},{13,15},{10,14},{15,... | collective-permute-start | bytes 589832 | tf_op jit(solution)/shard_map/ppermute | solution.py:262
  10.5 9.2 %collective-permute-start.5 = (f32[8,24,256]{2,1,0:T(8,128)S(1)}, f32[8,24,256]{2,1,0:T(8,128)S(1)}, u32[]{:S(2)}, u32[]{:S(2)}) collective-permute-start(f32[8,24,256]{2,1,0:T(8,128)S(1)} %collective-permute-done.4.refs_0_), channel_id=1, source_target_pairs={{0,4},{5,1},{4,8},{9,5},{8,12},{13,9},{12,14},{15,13},{14,10},{11,... | collective-permute-start | bytes 589832 | tf_op jit(solution)/shard_map/ppermute | solution.py:262
  14.7 6.8 %collective-permute-start.10 = (f32[8,24,256]{2,1,0:T(8,128)S(1)}, f32[8,24,256]{2,1,0:T(8,128)S(1)}, u32[]{:S(2)}, u32[]{:S(2)}) collective-permute-start(f32[8,24,256]{2,1,0:T(8,128)S(1)} %collective-permute-done.8.refs_0_), channel_id=1, source_target_pairs={{0,4},{5,1},{4,8},{9,5},{8,12},{13,9},{12,14},{15,13},{14,10},{11,... | collective-permute-start | bytes 589832 | tf_op jit(solution)/shard_map/ppermute | solution.py:262
  14.7 6.8 %collective-permute-start.11 = (f32[8,24,256]{2,1,0:T(8,128)S(1)}, f32[8,24,256]{2,1,0:T(8,128)S(1)}, u32[]{:S(2)}, u32[]{:S(2)}) collective-permute-start(f32[8,24,256]{2,1,0:T(8,128)S(1)} %collective-permute-done.9.refs_1_), channel_id=1, source_target_pairs={{4,0},{1,5},{8,4},{5,9},{12,8},{9,13},{14,12},{13,15},{10,14},{15,... | collective-permute-start | bytes 589832 | tf_op jit(solution)/shard_map/ppermute | solution.py:262
  17.6 9.1 %collective-permute-start.2 = (f32[8,24,256]{2,1,0:T(8,128)S(1)}, f32[8,24,256]{2,1,0:T(8,128)S(1)}, u32[]{:S(2)}, u32[]{:S(2)}) collective-permute-start(f32[8,24,256]{2,1,0:T(8,128)S(1)} %collective-permute-done.1.refs_1_), channel_id=1, source_target_pairs={{4,0},{1,5},{8,4},{5,9},{12,8},{9,13},{14,12},{13,15},{10,14},{15,... | collective-permute-start | bytes 589832 | tf_op jit(solution)/shard_map/ppermute | solution.py:262
  19.6 7.0 %collective-permute-start.6 = (f32[8,24,256]{2,1,0:T(8,128)S(1)}, f32[8,24,256]{2,1,0:T(8,128)S(1)}, u32[]{:S(2)}, u32[]{:S(2)}) collective-permute-start(f32[8,24,256]{2,1,0:T(8,128)S(1)} %collective-permute-done.5.refs_0_), channel_id=1, source_target_pairs={{0,4},{5,1},{4,8},{9,5},{8,12},{13,9},{12,14},{15,13},{14,10},{11,... | collective-permute-start | bytes 589832 | tf_op jit(solution)/shard_map/ppermute | solution.py:262
  21.5 8.3 %collective-permute-start.12 = (f32[8,24,256]{2,1,0:T(8,128)S(1)}, f32[8,24,256]{2,1,0:T(8,128)S(1)}, u32[]{:S(2)}, u32[]{:S(2)}) collective-permute-start(f32[8,24,256]{2,1,0:T(8,128)S(1)} %collective-permute-done.10.refs_0_), channel_id=1, source_target_pairs={{0,4},{5,1},{4,8},{9,5},{8,12},{13,9},{12,14},{15,13},{14,10},{11,... | collective-permute-start | bytes 589832 | tf_op jit(solution)/shard_map/ppermute | solution.py:262
  22.6 7.1 %collective-permute-start.13 = (f32[8,24,256]{2,1,0:T(8,128)S(1)}, f32[8,24,256]{2,1,0:T(8,128)S(1)}, u32[]{:S(2)}, u32[]{:S(2)}) collective-permute-start(f32[8,24,256]{2,1,0:T(8,128)S(1)} %collective-permute-done.11.refs_1_), channel_id=1, source_target_pairs={{4,0},{1,5},{8,4},{5,9},{12,8},{9,13},{14,12},{13,15},{10,14},{15,... | collective-permute-start | bytes 589832 | tf_op jit(solution)/shard_map/ppermute | solution.py:262
  26.6 6.2 %collective-permute-start.7 = (f32[8,24,256]{2,1,0:T(8,128)S(1)}, f32[8,24,256]{2,1,0:T(8,128)S(1)}, u32[]{:S(2)}, u32[]{:S(2)}) collective-permute-start(f32[8,24,256]{2,1,0:T(8,128)S(1)} %collective-permute-done.6.refs_0_), channel_id=1, source_target_pairs={{0,4},{5,1},{4,8},{9,5},{8,12},{13,9},{12,14},{15,13},{14,10},{11,... | collective-permute-start | bytes 589832 | tf_op jit(solution)/shard_map/ppermute | solution.py:262
  26.6 7.0 %collective-permute-start.3 = (f32[8,24,256]{2,1,0:T(8,128)S(1)}, f32[8,24,256]{2,1,0:T(8,128)S(1)}, u32[]{:S(2)}, u32[]{:S(2)}) collective-permute-start(f32[8,24,256]{2,1,0:T(8,128)S(1)} %collective-permute-done.2.refs_1_), channel_id=1, source_target_pairs={{4,0},{1,5},{8,4},{5,9},{12,8},{9,13},{14,12},{13,15},{10,14},{15,... | collective-permute-start | bytes 589832 | tf_op jit(solution)/shard_map/ppermute | solution.py:262
  33.5 5.2 %copy-start = (bf16[256,1024]{1,0:T(8,128)(2,1)S(1)}, bf16[256,1024]{1,0:T(8,128)(2,1)}, u32[]{:S(2)}) copy-start(bf16[256,1024]{1,0:T(8,128)(2,1)} %constant.17.clone.col_ref) | copy-start | bytes 1572868
  33.9 4.8 %collective-permute-start.14 = (f32[16,128]{1,0:T(8,128)S(1)}, f32[16,128]{1,0:T(8,128)S(1)}, u32[]{:S(2)}, u32[]{:S(2)}) collective-permute-start(f32[16,128]{1,0:T(8,128)S(1)} %get-tuple-element.30.mine_ref), channel_id=1, source_target_pairs={{0,1},{1,0},{2,3},{3,2},{4,5},{5,4},{6,7},{7,6},{8,9},{9,8},{10,11... | collective-permute-start | bytes 24584 | tf_op jit(solution)/shard_map/ppermute | solution.py:317
